TPU v7x, 32 devices: a whole 2x2x4 slice. The times are simulated.
32 devices in a mesh: dom: 8 (over y, x, core), mode: 4 (over z).
Axes of the slice: x: 2, y: 2, z: 4, core: 2. Of those that a mesh axis runs over, the one named last changes fastest.
Arguments:
- source: float32 [32768], P('dom'), may hold values from -36 to 36
- mass: float32 [32768], P('dom'), may hold values from 0.3 to 3
- lambdas: float32 [16], P('mode'), may hold values from 0.05 to 4
- trace_basis: float32 [16, 16], replicated, may hold values from -3 to 3
- blocks: float32 [9, 64, 32768], P(None, None, 'dom'), may hold values from -0.01 to 2, as said below
- columns: int32 [512, 9], P('dom'), may hold values from 0 to 191, as said below
Outputs:
- trace_levels: float32 [16, 32768], P('mode', 'dom')
Inputs may be any that keep to these rules, and one draw needn't show every extreme that they name: `columns`: slot 0 of cluster c names c itself; slots 1 to 4 name clusters of the same partition, or c itself where the block is zero; slot 5 + h names 64 + h * 32 + c when c < 32 and cluster c is coupled to cluster c of partition p + (-2, -1, 1, 2)[h], else c itself with a zero block. The number of coupled partitions differs between partitions. The pattern is symmetric. The operator assembled from blocks and columns is symmetric and strictly diagonally dominant with a positive diagonal.
All inputs are finite; a program needn't handle non-finite values.
Results may differ from a plain program's by a relative error of at most 0.00015.
Values sent between devices are 32-bit elements; how exact they have to be, the bound alone decides.
A program may use at most 128 MiB of HBM per device.

v0:
```python
import jax
import jax.numpy as jnp
from jax import lax
from jax.sharding import PartitionSpec as P

LEVELS = 16
ITERS = 2


OFFSETS = (-2, -1, 1, 2)
HIGHEST = lax.Precision.HIGHEST


def passed_along(block, axis, distance):
    devices = range(lax.axis_size(axis))
    route = [((i - distance) % len(devices), i) for i in devices]
    return lax.ppermute(block, axis, route)


def contract(weights, gathered):
    return jnp.einsum("sjci,mcsj->mci", weights, gathered, precision=HIGHEST)


def apply_operator(field, blocks, columns, shift_field):
    modes_dev, vertices = field.shape
    clusters = columns.shape[0]
    block_width = blocks.shape[1]
    shared = clusters // 2
    pieces = field.reshape(modes_dev, clusters, block_width)
    weights = blocks.reshape(blocks.shape[0], block_width, clusters, block_width)
    interior = contract(weights[:5], pieces[:, columns[:, :5], :])
    border = pieces[:, :shared, :].reshape(modes_dev, shared * block_width)
    borders_in = [passed_along(border, "dom", -offset) for offset in OFFSETS]
    extended = jnp.concatenate(
        [pieces] + [piece.reshape(modes_dev, shared, block_width) for piece in borders_in], axis=1
    )
    exterior = contract(weights[5:], extended[:, columns[:, 5:], :])
    return (interior + exterior).reshape(modes_dev, vertices) + shift_field * field


def squares(residual):
    return lax.psum(jnp.sum(residual * residual, axis=1), "dom")


def body(source, mass, lambdas, trace_basis, blocks, columns):
    modes_dev = lambdas.shape[0]
    mode_index = lax.axis_index("mode")
    levels_dev = LEVELS // lax.axis_size("mode")
    rhs_weight = lax.dynamic_slice_in_dim(trace_basis[0], mode_index * modes_dev, modes_dev)
    shift_field = lambdas[:, None] * mass[None, :]
    right_side = rhs_weight[:, None] * (mass * source)[None, :]
    solution = jnp.zeros_like(right_side)
    residual = right_side
    direction = right_side
    norm_now = squares(residual)
    for number in range(ITERS):
        image = apply_operator(direction, blocks, columns, shift_field)
        curvature = lax.psum(jnp.sum(direction * image, axis=1), "dom")
        step_size = norm_now / curvature
        solution = solution + step_size[:, None] * direction
        if number + 1 < ITERS:
            residual = residual - step_size[:, None] * image
            norm_next = squares(residual)
            direction = residual + (norm_next / norm_now)[:, None] * direction
            norm_now = norm_next
    every_mode = lax.all_gather(solution, "mode", axis=0, tiled=True)
    level_rows = lax.dynamic_slice_in_dim(trace_basis, mode_index * levels_dev, levels_dev, 0)
    result = jnp.dot(level_rows, every_mode, precision=HIGHEST)
    return result


def solution(mesh):
    in_specs = (P("dom"), P("dom"), P("mode"), P(), P(None, None, "dom"), P("dom", None))
    out_specs = P("mode", "dom")
    return jax.shard_map(body, mesh=mesh, in_specs=in_specs, out_specs=out_specs, check_vma=False)
```

profile of v0, /device:TPU:0, one launch (start us, length us, event | category | flops | bytes accessed | tf_op | source)
XLA Modules:
  0.0 159.7 jit_solution(12525032145836400519)
XLA Ops:
  0.0 0.7 slice.31
  0.7 0.7 mul.134
  1.8 3.0 %collective-permute-start = (f32[4,2048]{1,0:T(4,128)S(1)}, f32[4,2048]{1,0:T(4,128)S(1)}, u32[]{:S(2)}, u32[]{:S(2)}) collective-permute-start(f32[4,2048]{1,0:T(4,128)S(1)} %reshape.149), channel_id=1, source_target_pairs={{24,0},{28,4},{0,8},{4,12},{8,16},{12,20},{16,24},{20,28},{25,1},{... | collective-permute-start | bytes 98312 | tf_op jit(solution)/shard_map/ppermute | solution.py:17
  4.8 2.6 %collective-permute-start.2 = (f32[4,2048]{1,0:T(4,128)S(1)}, f32[4,2048]{1,0:T(4,128)S(1)}, u32[]{:S(2)}, u32[]{:S(2)}) collective-permute-start(f32[4,2048]{1,0:T(4,128)S(1)} %reshape.149), channel_id=1, source_target_pairs={{4,0},{8,4},{12,8},{16,12},{20,16},{24,20},{28,24},{0,28},{5,1},{9... | collective-permute-start | bytes 98312 | tf_op jit(solution)/shard_map/ppermute | solution.py:17
  7.4 0.1 collective-permute-start.3
  7.6 0.7 compare_select_fusion.1
  8.3 0.7 compare_select_fusion
  9.0 0.2 fusion.44
  9.5 0.1 reshape.162
  9.6 4.6 %slice.37 = f32[4,64,4096]{2,1,0:T(8,128)} slice(f32[9,64,4096]{2,1,0:T(8,128)} %param.10), slice={[5:9], [0:64], [0:4096]} | slice | bytes 8388608 | tf_op jit(solution)/shard_map/slice | solution.py:37
  14.2 5.4 %slice.33 = f32[5,64,4096]{2,1,0:T(8,128)} slice(f32[9,64,4096]{2,1,0:T(8,128)} %param.10), slice={[0:5], [0:64], [0:4096]} | slice | bytes 10485760 | tf_op jit(solution)/shard_map/slice | solution.py:31
  19.7 7.9 %slice.38 = f32[4,64,64,64]{3,2,1,0:T(8,128)} reshape(f32[4,64,4096]{2,1,0:T(8,128)} %slice.37) | data formatting | bytes 8388608 | tf_op jit(solution)/shard_map/slice | solution.py:37
  27.6 2.0 %gather_fusion = f32[320,4,64]{2,1,0:T(4,128)S(1)} fusion(f32[4,64,64]{2,0,1:T(4,128)S(1)} %get-tuple-element.11, s32[1024]{0:T(1024)S(1)} %pad_clamp_fusion.1), kind=kCustom, calls=%fused_computation | custom fusion | bytes 656640 | tf_op jit(solution)/shard_map/gather | solution.py:31
  29.6 9.4 %slice.34 = f32[5,64,64,64]{3,2,1,0:T(8,128)} reshape(f32[5,64,4096]{2,1,0:T(8,128)} %slice.33) | data formatting | bytes 10485760 | tf_op jit(solution)/shard_map/slice | solution.py:31
  39.7 1.0 gather_fusion.1
  40.7 12.5 %fusion.8 = f32[64,4,64]{2,1,0:T(4,128)S(1)} fusion(f32[4,64,4,64]{3,0,2,1:T(4,128)S(1)} %bitcast.60, f32[4,64,64,64]{3,2,1,0:T(8,128)} %slice.38), kind=kOutput, calls=%fused_computation.12 | convolution fusion | flops 50331648 | bytes 4521984 | tf_op jit(solution)/shard_map/sjci,mcsj->mci/dot_general | solution.py:21
  53.2 16.4 %fusion.42 = (f32[4]{0:T(128)S(1)}, f32[4,64,64]{2,0,1:T(4,128)S(1)}, f32[4,64,64]{2,0,1:T(4,128)S(1)}) fusion(f32[64,64]{1,0:T(8,128)S(1)} %mul.139, f32[4]{0:T(128)S(1)} %dynamic-slice_bitcast_fusion, f32[64,64]{1,0:T(8,128)S(1)} %mul.143, f32[4]{0:T(128)S(1)} %copy-done.1, f32[64,4,64]{2,1,0:T(4,128)S(1)} %fusion.8, f32[4,64,5,64]{3,0,2,1:T(4,128)S(1)} %bitcast.58, ...), kind=kOutput, calls=%fused_computation.35 | convolution fusion | flops 63029244 | bytes 5799984 | tf_op jit(solution)/shard_map/sjci,mcsj->mci/dot_general | solution.py:21
  69.6 11.8 %all-reduce = (f32[4]{0:T(128)S(1)}, f32[4]{0:T(128)S(1)}) all-reduce(f32[4]{0:T(128)S(1)} %fusion.44, f32[4]{0:T(128)S(1)} %get-tuple-element.9), channel_id=1, replica_groups=mesh['dom'=8,'mode'=4] {'dom'}, use_global_device_ids=true, to_apply=%region_1.0 | all-reduce | flops 8 | bytes 64 | tf_op jit(solution)/shard_map/psum | solution.py:42
  81.4 0.3 multiply_reduce_fusion
  81.7 12.3 %psum.30 = f32[4]{0:T(128)S(1)} all-reduce(f32[4]{0:T(128)S(1)} %multiply_reduce_fusion), channel_id=1, replica_groups=mesh['dom'=8,'mode'=4] {'dom'}, use_global_device_ids=true, to_apply=%region_5.0 | all-reduce | flops 4 | bytes 32 | tf_op jit(solution)/shard_map/psum | solution.py:42
  94.0 0.1 constant_dynamic-update-slice_fusion
  94.4 2.6 %collective-permute-start.6 = (f32[4,2048]{1,0:T(4,128)S(1)}, f32[4,2048]{1,0:T(4,128)S(1)}, u32[]{:S(2)}, u32[]{:S(2)}) collective-permute-start(f32[4,2048]{1,0:T(4,128)S(1)} %reshape.154), channel_id=1, source_target_pairs={{4,0},{8,4},{12,8},{16,12},{20,16},{24,20},{28,24},{0,28},{5,1},{9... | collective-permute-start | bytes 98312 | tf_op jit(solution)/shard_map/ppermute | solution.py:17
  97.0 2.0 %collective-permute-start.7 = (f32[4,2048]{1,0:T(4,128)S(1)}, f32[4,2048]{1,0:T(4,128)S(1)}, u32[]{:S(2)}, u32[]{:S(2)}) collective-permute-start(f32[4,2048]{1,0:T(4,128)S(1)} %reshape.154), channel_id=1, source_target_pairs={{8,0},{12,4},{16,8},{20,12},{24,16},{28,20},{0,24},{4,28},{9,1},{1... | collective-permute-start | bytes 98312 | tf_op jit(solution)/shard_map/ppermute | solution.py:17
  99.0 2.2 %gather_fusion.2 = f32[320,4,64]{2,1,0:T(4,128)S(1)} fusion(f32[4,64,64]{2,0,1:T(4,128)S(1)} %get-tuple-element.8, s32[1024]{0:T(1024)S(1)} %pad_clamp_fusion.1), kind=kCustom, calls=%fused_computation.2 | custom fusion | bytes 656640 | tf_op jit(solution)/shard_map/gather | solution.py:31
  101.9 1.0 gather_fusion.3
  102.9 12.5 %fusion.11 = f32[64,4,64]{2,1,0:T(4,128)S(1)} fusion(f32[4,64,4,64]{3,0,2,1:T(4,128)S(1)} %bitcast.59, f32[4,64,64,64]{3,2,1,0:T(8,128)} %slice.38), kind=kOutput, calls=%fused_computation.13 | convolution fusion | flops 50331648 | bytes 4521984 | tf_op jit(solution)/shard_map/sjci,mcsj->mci/dot_general | solution.py:21
  115.4 16.4 %fusion.38 = f32[4]{0:T(128)S(1)} fusion(f32[4,64,64]{2,0,1:T(4,128)S(1)} %get-tuple-element.8, f32[64,4,64]{2,1,0:T(4,128)S(1)} %fusion.11, f32[4,64,5,64]{3,0,2,1:T(4,128)S(1)} %bitcast.57, f32[5,64,64,64]{3,2,1,0:T(8,128)} %slice.34, f32[64,64]{1,0:T(8,128)S(1)} %mul.143, f32[4]{0:T(128)S(1)} %copy-done.1), kind=kOutput, calls=%fused_computation.22 | convolution fusion | flops 63012860 | bytes 5718048 | tf_op jit(solution)/shard_map/sjci,mcsj->mci/dot_general | solution.py:21
  131.9 0.1 reshape.159
  132.0 11.8 %psum.31 = f32[4]{0:T(128)S(1)} all-reduce(f32[4]{0:T(128)S(1)} %fusion.38), channel_id=1, replica_groups=mesh['dom'=8,'mode'=4] {'dom'}, use_global_device_ids=true, to_apply=%region_7.0 | all-reduce | flops 4 | bytes 32 | tf_op jit(solution)/shard_map/psum | solution.py:58
  143.8 0.1 fusion.46
  143.9 14.1 %all-gather = f32[4,4,4096]{2,1,0:T(4,128)S(1)} all-gather(f32[1,4,4096]{2,1,0:T(4,128)S(1)} %fusion.46), channel_id=1, replica_groups=mesh['dom'=8,'mode'=4] {'mode'}, dimensions={0}, use_global_device_ids=true | all-gather | bytes 327680 | tf_op jit(solution)/shard_map/all_gather | solution.py:66
  158.1 1.6 fusion.51
  (51 shorter events, 2.3 us)
Async XLA Ops:
  1.8 37.2 %collective-permute-start = (f32[4,2048]{1,0:T(4,128)S(1)}, f32[4,2048]{1,0:T(4,128)S(1)}, u32[]{:S(2)}, u32[]{:S(2)}) collective-permute-start(f32[4,2048]{1,0:T(4,128)S(1)} %reshape.149), channel_id=1, source_target_pairs={{24,0},{28,4},{0,8},{4,12},{8,16},{12,20},{16,24},{20,28},{25,1},{... | collective-permute-start | bytes 98312 | tf_op jit(solution)/shard_map/ppermute | solution.py:17
  4.8 34.4 %collective-permute-start.1 = (f32[4,2048]{1,0:T(4,128)S(1)}, f32[4,2048]{1,0:T(4,128)S(1)}, u32[]{:S(2)}, u32[]{:S(2)}) collective-permute-start(f32[4,2048]{1,0:T(4,128)S(1)} %reshape.149), channel_id=1, source_target_pairs={{28,0},{0,4},{4,8},{8,12},{12,16},{16,20},{20,24},{24,28},{29,1},{... | collective-permute-start | bytes 98312 | tf_op jit(solution)/shard_map/ppermute | solution.py:17
  4.8 34.5 %collective-permute-start.2 = (f32[4,2048]{1,0:T(4,128)S(1)}, f32[4,2048]{1,0:T(4,128)S(1)}, u32[]{:S(2)}, u32[]{:S(2)}) collective-permute-start(f32[4,2048]{1,0:T(4,128)S(1)} %reshape.149), channel_id=1, source_target_pairs={{4,0},{8,4},{12,8},{16,12},{20,16},{24,20},{28,24},{0,28},{5,1},{9... | collective-permute-start | bytes 98312 | tf_op jit(solution)/shard_map/ppermute | solution.py:17
  7.4 32.1 %collective-permute-start.3 = (f32[4,2048]{1,0:T(4,128)S(1)}, f32[4,2048]{1,0:T(4,128)S(1)}, u32[]{:S(2)}, u32[]{:S(2)}) collective-permute-start(f32[4,2048]{1,0:T(4,128)S(1)} %reshape.149), channel_id=1, source_target_pairs={{8,0},{12,4},{16,8},{20,12},{24,16},{28,20},{0,24},{4,28},{9,1},{1... | collective-permute-start | bytes 98312 | tf_op jit(solution)/shard_map/ppermute | solution.py:17
  9.6 10.0 %copy-start = (f32[4096]{0:T(1024)S(1)}, f32[4096]{0:T(1024)}, u32[]{:S(2)}) copy-start(f32[4096]{0:T(1024)} %param.7) | copy-start | bytes 49156
  39.0 14.2 %copy-start.1 = (f32[4]{0:T(128)S(1)}, f32[4]{0:T(128)}, u32[]{:S(2)}) copy-start(f32[4]{0:T(128)} %param.8) | copy-start | bytes 52
  94.3 7.0 %collective-permute-start.4 = (f32[4,2048]{1,0:T(4,128)S(1)}, f32[4,2048]{1,0:T(4,128)S(1)}, u32[]{:S(2)}, u32[]{:S(2)}) collective-permute-start(f32[4,2048]{1,0:T(4,128)S(1)} %reshape.154), channel_id=1, source_target_pairs={{24,0},{28,4},{0,8},{4,12},{8,16},{12,20},{16,24},{20,28},{25,1},{... | collective-permute-start | bytes 98312 | tf_op jit(solution)/shard_map/ppermute | solution.py:17
  94.3 7.1 %collective-permute-start.5 = (f32[4,2048]{1,0:T(4,128)S(1)}, f32[4,2048]{1,0:T(4,128)S(1)}, u32[]{:S(2)}, u32[]{:S(2)}) collective-permute-start(f32[4,2048]{1,0:T(4,128)S(1)} %reshape.154), channel_id=1, source_target_pairs={{28,0},{0,4},{4,8},{8,12},{12,16},{16,20},{20,24},{24,28},{29,1},{... | collective-permute-start | bytes 98312 | tf_op jit(solution)/shard_map/ppermute | solution.py:17
  94.4 7.2 %collective-permute-start.6 = (f32[4,2048]{1,0:T(4,128)S(1)}, f32[4,2048]{1,0:T(4,128)S(1)}, u32[]{:S(2)}, u32[]{:S(2)}) collective-permute-start(f32[4,2048]{1,0:T(4,128)S(1)} %reshape.154), channel_id=1, source_target_pairs={{4,0},{8,4},{12,8},{16,12},{20,16},{24,20},{28,24},{0,28},{5,1},{9... | collective-permute-start | bytes 98312 | tf_op jit(solution)/shard_map/ppermute | solution.py:17
  97.0 4.7 %collective-permute-start.7 = (f32[4,2048]{1,0:T(4,128)S(1)}, f32[4,2048]{1,0:T(4,128)S(1)}, u32[]{:S(2)}, u32[]{:S(2)}) collective-permute-start(f32[4,2048]{1,0:T(4,128)S(1)} %reshape.154), channel_id=1, source_target_pairs={{8,0},{12,4},{16,8},{20,12},{24,16},{28,20},{0,24},{4,28},{9,1},{1... | collective-permute-start | bytes 98312 | tf_op jit(solution)/shard_map/ppermute | solution.py:17
where the time goes:
time: 160 us
  matrix products  59.5 us (37%)
  blocking collectives  50.1 us (31%)
  local copies, waits for them, and re-layouts  36.5 us (23%)
  starting transfers between devices  10.5 us (7%)
  other arithmetic  2.99 us (2%)
    dot_general x4, matrix products, contract(): return jnp.einsum('sjci,mcsj->mci', weights, gathered, precision=HIGHEST)  57.9 us
    psum x2, blocking collectives, squares(): return lax.psum(jnp.sum(residual * residual, axis=1), 'dom')  24.2 us
    slice x2, local copies, waits for them, and re-layouts, apply_operator(): interior = contract(weights[:5], pieces[:, columns[:, :5], :])  14.8 us
    all_gather x1, blocking collectives, body(): every_mode = lax.all_gather(solution, 'mode', axis=0, tiled=True)  14.1 us
    slice x2, local copies, waits for them, and re-layouts, apply_operator(): exterior = contract(weights[5:], extended[:, columns[:, 5:], :])  12.4 us
    psum x1, blocking collectives, body(): curvature = lax.psum(jnp.sum(direction * image, axis=1), 'dom')  11.8 us
    ppermute x8, starting transfers between devices, passed_along(): return lax.ppermute(block, axis, route)  10.5 us
    gather x2, local copies, waits for them, and re-layouts, apply_operator(): interior = contract(weights[:5], pieces[:, columns[:, :5], :])  4.2 us
  transfers between devices with their start and end apart: 8, of which 0 were waited for; matrix products, arithmetic and copies ran while one was open for 22% of the time, Pallas kernels for 0%

commit v1 on v0

v1 whole, which is shorter than its diff:
```python
import functools

import jax
import jax.numpy as jnp
from jax import lax
from jax.experimental import pallas as pl
from jax.experimental.pallas import tpu as pltpu
from jax.sharding import PartitionSpec as P

LEVELS = 16
OFFSETS = (-2, -1, 1, 2)
OWN = 5
HIGHEST = lax.Precision.HIGHEST
MESH = pl.DeviceIdType.MESH
F32 = jnp.float32
BF16 = jnp.bfloat16


def halves(value):
    high = value.astype(BF16)
    return high, (value - high.astype(F32)).astype(BF16)


def dot(a, b, dims=((1,), (0,)), precision=None):
    return lax.dot_general(a, b, (dims, ((), ())), precision=precision, preferred_element_type=F32)


def fold(value):
    half = value.shape[0] // 2
    return jnp.concatenate([value[:half], value[half:]], axis=1)


def unfold(value):
    half = value.shape[1] // 2
    return jnp.concatenate([value[:, :half], value[:, half:]], axis=0)


def column_of(row):
    n = row.shape[1]
    eye = lax.broadcasted_iota(jnp.int32, (n, n), 0) == lax.broadcasted_iota(jnp.int32, (n, n), 1)
    spread = jnp.where(eye, jnp.broadcast_to(row, (n, n)), 0.0)
    return jnp.broadcast_to(jnp.sum(spread, axis=1, keepdims=True), (n, 128))


def kernel(
    n_dom, n_mode,
    source_ref, mass_ref, lam_ref, basis_ref, blocks_ref, cols_ref, out_ref,
    own_f32, far_f32, own_hi, own_lo, far_hi, far_lo, v_ref, acc_own, acc_far,
    lam_buf, far1_out, far1_in, far2_out, far2_in, sum1_out, sum1_in, sum2_out, sum2_in,
    load_sem, lam_send, lam_recv, far1_send, far1_recv, far2_send, far2_recv,
    sum1_send, sum1_recv, sum2_send, sum2_recv,
):
    me = lax.axis_index("dom")
    my_mode = lax.axis_index("mode")
    width = own_f32.shape[1]
    clusters = cols_ref.shape[0]
    shared = clusters // 2
    md = lam_ref.shape[1]
    levels = out_ref.shape[1]
    span = 1024
    far_chunks = shared * width // span
    own_chunks = clusters * width // span
    per_chunk = span // width

    loads = []
    for n in range(far_chunks):
        lanes = pl.ds(n * span, span)
        loads.append(pltpu.make_async_copy(
            blocks_ref.at[pl.ds(OWN, 4), :, lanes], far_f32.at[:, :, lanes], load_sem.at[n]))
    for n in range(own_chunks):
        lanes = pl.ds(n * span, span)
        loads.append(pltpu.make_async_copy(
            blocks_ref.at[pl.ds(0, OWN), :, lanes], own_f32.at[:, :, lanes], load_sem.at[far_chunks + n]))
    for load in loads:
        load.start()

    barrier = pltpu.get_barrier_semaphore()
    for d in range(1, n_dom):
        pl.semaphore_signal(barrier, inc=1, device_id=(lax.rem(me + d, n_dom), my_mode), device_id_type=MESH)
    for d in range(1, n_mode):
        pl.semaphore_signal(barrier, inc=1, device_id=(me, lax.rem(my_mode + d, n_mode)), device_id_type=MESH)

    f_nat = mass_ref[...] * source_ref[...]
    m_nat = mass_ref[...]
    w_nat = m_nat * f_nat
    pairs = clusters // 2
    pair_row = lax.broadcasted_iota(jnp.int32, (pairs, clusters), 0)
    cluster_col = lax.broadcasted_iota(jnp.int32, (pairs, clusters), 1)
    even = (cluster_col == 2 * pair_row).astype(F32)
    odd = (cluster_col == 2 * pair_row + 1).astype(F32)

    def across(nat):
        first = dot(nat, even, ((0,), (0,)), HIGHEST)
        second = dot(nat, odd, ((0,), (0,)), HIGHEST)
        return first[:width] + second[width:]

    def back(vec):
        first = dot(even, vec, ((1,), (1,)), HIGHEST)
        second = dot(odd, vec, ((1,), (1,)), HIGHEST)
        return jnp.concatenate([first, second], axis=1)

    m_t = across(m_nat)
    f_t = across(f_nat)
    w_t = m_t * f_t

    def spread(vectors):
        high = [v.astype(BF16).astype(F32) for v in vectors]
        packed = jnp.concatenate(high + [v - h for v, h in zip(vectors, high)], axis=1)
        lane = lax.rem(lax.broadcasted_iota(jnp.int32, packed.shape, 1), clusters)
        n = packed.shape[1]

        def place(g, carry):
            v_ref[pl.ds(pl.multiple_of(g * width, width), width), 0:n] = jnp.where(lane == g, packed, 0.0).astype(BF16)
            return carry
        lax.fori_loop(0, clusters, place, 0, unroll=8)

    spread([f_t, w_t])

    lam_row = lam_ref[...]
    lam_tile = jnp.concatenate([column_of(lam_row), jnp.zeros((8 - md, 128), F32)], axis=0)
    lam_buf[0] = lam_tile
    wait_for = n_dom - 1 + n_mode - 1
    pl.semaphore_wait(barrier, wait_for)

    sends = []
    lam_copies = []
    for d in range(1, n_mode):
        copy = pltpu.make_async_remote_copy(
            src_ref=lam_buf.at[0], dst_ref=lam_buf.at[d], send_sem=lam_send.at[d], recv_sem=lam_recv.at[d],
            device_id=(me, lax.rem(my_mode + d, n_mode)), device_id_type=MESH)
        copy.start()
        lam_copies.append(copy)

    def far_copies(out_buf, in_buf, send, recv):
        copies = []
        for h, offset in enumerate(OFFSETS):
            copies.append(pltpu.make_async_remote_copy(
                src_ref=out_buf.at[h], dst_ref=in_buf.at[h], send_sem=send.at[h], recv_sem=recv.at[h],
                device_id=(lax.rem(me + n_dom + offset, n_dom), my_mode), device_id_type=MESH))
        return copies

    def sum_copies(out_buf, in_buf, send, recv):
        copies = []
        for d in range(1, n_dom):
            copies.append(pltpu.make_async_remote_copy(
                src_ref=out_buf, dst_ref=in_buf.at[d - 1], send_sem=send.at[d - 1], recv_sem=recv.at[d - 1],
                device_id=(lax.rem(me + d, n_dom), my_mode), device_id_type=MESH))
        return copies

    def product(count, chunks, first_load, full, high, low, acc, n, first_pass):
        for c in range(chunks):
            lanes = pl.ds(c * span, span)
            if first_pass:
                loads[first_load + c].wait()
                hi, lo = halves(full[:, :, lanes].reshape(count * width, span))
                high[:, lanes] = hi
                low[:, lanes] = lo
            else:
                hi, lo = high[:, lanes], low[:, lanes]
            right = v_ref[lanes, 0:n]
            part = dot(hi, right) + dot(lo, right)
            if c:
                acc[:, 0:n] += part
            else:
                acc[:, 0:n] = part
        return acc[:, 0:n // 2] + acc[:, n // 2:n]

    cluster_lane = lax.broadcasted_iota(jnp.int32, (clusters, clusters), 1)

    def collect(terms, vectors):
        total = terms[:width]
        high, low = halves(terms[width:])
        moved = None
        for s in range(1, OWN):
            hot = (cols_ref[:, s:s + 1] == cluster_lane).astype(F32).astype(BF16)
            if vectors == 2:
                zero = jnp.zeros_like(hot)
                hot = jnp.concatenate([jnp.concatenate([hot, zero], 1), jnp.concatenate([zero, hot], 1)], 0)
            rows = slice((s - 1) * width, s * width)
            part = dot(high[rows], hot) + dot(low[rows], hot)
            moved = part if moved is None else moved + part
        return total + moved

    def widen(value):
        return jnp.concatenate([value, jnp.zeros((width, clusters - shared), F32)], axis=1)

    n1 = 4 * clusters
    terms = product(4, far_chunks, 0, far_f32, far_hi, far_lo, acc_far, n1, True)
    far1 = far_copies(far1_out, far1_in, far1_send, far1_recv)
    for h in range(4):
        rows = terms[h * width:(h + 1) * width]
        both = jnp.concatenate([rows[:, :shared], rows[:, clusters:clusters + shared]], axis=1)
        far1_out[h] = fold(both)
        far1[h].start()
    terms = product(OWN, own_chunks, far_chunks, own_f32, own_hi, own_lo, acc_own, n1, True)
    image = collect(terms, 2)
    for h in range(4):
        far1[h].wait_recv()
    arrived = unfold(far1_in[0] + far1_in[1] + far1_in[2] + far1_in[3])
    u_t = image[:, :clusters] + widen(arrived[:, :shared])
    q_t = image[:, clusters:] + widen(arrived[:, shared:])

    f_v, w_v, m_v, u_v, q_v = fold(f_t), fold(w_t), fold(m_t), fold(u_t), fold(q_t)

    def over(value):
        return jnp.sum(value, axis=0, keepdims=True)

    sum1_out[...] = jnp.concatenate(
        [over(f_v * f_v), over(f_v * u_v), over(f_v * w_v), jnp.zeros((5, 128), F32)], axis=0)
    sum1 = sum_copies(sum1_out, sum1_in, sum1_send, sum1_recv)
    for copy in sum1:
        copy.start()

    n2 = 2 * clusters
    spread([u_t])
    terms = product(4, far_chunks, 0, far_f32, far_hi, far_lo, acc_far, n2, False)
    far2 = far_copies(far2_out, far2_in, far2_send, far2_recv)
    for h in range(4):
        far2_out[h] = fold(fold(terms[h * width:(h + 1) * width, :shared]))
        far2[h].start()
    terms = product(OWN, own_chunks, far_chunks, own_f32, own_hi, own_lo, acc_own, n2, False)
    image = collect(terms, 1)

    for copy in lam_copies:
        copy.wait_recv()
    lam = jnp.zeros((md * n_mode, 128), F32)
    part_row = lax.broadcasted_iota(jnp.int32, (md * n_mode, 128), 0) // md
    for d in range(n_mode):
        own = lax.rem(my_mode + n_mode - d, n_mode)
        tiled = jnp.concatenate([lam_buf[d][:md]] * n_mode, axis=0)
        lam = jnp.where(part_row == own, tiled, lam)
    t = column_of(basis_ref[0:1, :])
    t2 = t * t

    for copy in sum1:
        copy.wait_recv()
    sums = sum1_out[...]
    for d in range(n_dom - 1):
        sums = sums + sum1_in[d]
    sums = jnp.broadcast_to(jnp.sum(sums, axis=1, keepdims=True), (8, 128))
    rr0 = t2 * sums[0:1]
    alpha = rr0 / (t2 * (sums[1:2] + lam * sums[2:3]))
    alpha_lam = alpha * lam

    for h in range(4):
        far2[h].wait_recv()
    arrived = unfold(unfold(far2_in[0] + far2_in[1] + far2_in[2] + far2_in[3]))
    p_v = fold(image + widen(arrived))

    squares, curves = [], []
    for k in range(md * n_mode):
        a, al = alpha[k:k + 1], alpha_lam[k:k + 1]
        r = f_v - a * u_v - al * w_v
        image_r = u_v - a * p_v - al * q_v + lam[k:k + 1] * (m_v * r)
        squares.append(over(r * r))
        curves.append(over(r * image_r))
    sum2_out[...] = jnp.concatenate(squares + curves, axis=0)
    sum2 = sum_copies(sum2_out, sum2_in, sum2_send, sum2_recv)
    for copy in sum2:
        copy.start()

    u_nat = back(u_t)
    rows = [column_of(basis_ref[pl.ds(my_mode * levels + level, 1), :]) for level in range(levels)]

    for copy in sum2:
        copy.wait_recv()
    sums = sum2_out[...]
    for d in range(n_dom - 1):
        sums = sums + sum2_in[d]
    modes = md * n_mode
    sums = jnp.broadcast_to(jnp.sum(sums, axis=1, keepdims=True), (2 * modes, 128))
    rr1 = t2 * sums[:modes]
    beta = rr1 / rr0
    alpha1 = rr1 / (t2 * sums[modes:] - beta * (rr1 / alpha))
    coef_f = t * (alpha + alpha1 * (1.0 + beta))
    coef_u = -t * (alpha1 * alpha)
    coef_w = coef_u * lam
    for level in range(levels):
        c_f, c_u, c_w = (over(rows[level] * c) for c in (coef_f, coef_u, coef_w))
        out_ref[:, level, :] = c_f * f_nat + c_u * u_nat + c_w * w_nat

    for copy in lam_copies + far1 + far2 + sum1 + sum2:
        copy.wait_send()


def solution(mesh):
    n_dom, n_mode = mesh.shape["dom"], mesh.shape["mode"]

    def body(source, mass, lambdas, trace_basis, blocks, columns):
        slots, width, vertices = blocks.shape
        clusters = columns.shape[0]
        shared = clusters // 2
        md = lambdas.shape[0]
        levels = LEVELS // n_mode
        lines = vertices // 128
        vmem = pl.BlockSpec(memory_space=pltpu.VMEM)
        dma = pltpu.SemaphoreType.DMA
        chunks = vertices // 1024 + shared * width // 1024
        result = pl.pallas_call(
            functools.partial(kernel, n_dom, n_mode),
            out_shape=jax.ShapeDtypeStruct((lines, levels, 128), F32),
            in_specs=[vmem, vmem, vmem, vmem, pl.BlockSpec(memory_space=pl.ANY), vmem],
            out_specs=vmem,
            scratch_shapes=[
                pltpu.VMEM((OWN, width, vertices), F32),
                pltpu.VMEM((slots - OWN, width, shared * width), F32),
                pltpu.VMEM((OWN * width, vertices), BF16),
                pltpu.VMEM((OWN * width, vertices), BF16),
                pltpu.VMEM(((slots - OWN) * width, shared * width), BF16),
                pltpu.VMEM(((slots - OWN) * width, shared * width), BF16),
                pltpu.VMEM((vertices, 4 * clusters), BF16),
                pltpu.VMEM((OWN * width, 4 * clusters), F32),
                pltpu.VMEM(((slots - OWN) * width, 4 * clusters), F32),
                pltpu.VMEM((n_mode, 8, 128), F32),
                pltpu.VMEM((4, width // 2, 2 * clusters), F32),
                pltpu.VMEM((4, width // 2, 2 * clusters), F32),
                pltpu.VMEM((4, width // 4, 4 * shared), F32),
                pltpu.VMEM((4, width // 4, 4 * shared), F32),
                pltpu.VMEM((8, 128), F32),
                pltpu.VMEM((n_dom - 1, 8, 128), F32),
                pltpu.VMEM((2 * md * n_mode, 128), F32),
                pltpu.VMEM((n_dom - 1, 2 * md * n_mode, 128), F32),
                dma((chunks,)),
                dma((n_mode,)), dma((n_mode,)),
                dma((4,)), dma((4,)), dma((4,)), dma((4,)),
                dma((n_dom - 1,)), dma((n_dom - 1,)), dma((n_dom - 1,)), dma((n_dom - 1,)),
            ],
            compiler_params=pltpu.CompilerParams(
                collective_id=0, has_side_effects=True, vmem_limit_bytes=48 * 1024 * 1024),
        )(
            source.reshape(lines, 128), mass.reshape(lines, 128), lambdas.reshape(1, md),
            trace_basis, blocks, columns,
        )
        return jnp.transpose(result, (1, 0, 2)).reshape(levels, vertices)

    in_specs = (P("dom"), P("dom"), P("mode"), P(), P(None, None, "dom"), P("dom", None))
    return jax.shard_map(body, mesh=mesh, in_specs=in_specs, out_specs=P("mode", "dom"), check_vma=False)
```

time: 160 us -> 24.9 us (0.16)
  matrix products: 59.5 us -> 0 us
  blocking collectives: 50.1 us -> 0 us
  local copies, waits for them, and re-layouts: 36.5 us -> 4.2 us
  Pallas kernels: 0 us -> 20.2 us
  starting transfers between devices: 10.5 us -> 0 us
  other arithmetic: 2.99 us -> 0 us
    dot_general x5 -> x0, matrix products: 59.5 us -> none  [the longest x4 57.9 us: contract(): return jnp.einsum('sjci,mcsj->mci', weights, gathered, precision=HIGHEST)]
    psum x3 -> x0, blocking collectives: 36 us -> none  [the longest x2 24.2 us: squares(): return lax.psum(jnp.sum(residual * residual, axis=1), 'dom')]
    slice x9 -> x0, local copies, waits for them, and re-layouts: 28 us -> none  [the longest x2 14.8 us: apply_operator(): interior = contract(weights[:5], pieces[:, columns[:, :5], :])]
    pallas_call x0 -> x1, Pallas kernels: none -> 20.2 us  [body(): pl.pallas_call(functools.partial(kernel, n_dom, n_mode), out_shape=jax.Sh...]
    all_gather x1 -> x0, blocking collectives: 14.1 us -> none  [body(): every_mode = lax.all_gather(solution, 'mode', axis=0, tiled=True)]
    ppermute x8 -> x0, starting transfers between devices: 10.5 us -> none  [passed_along(): return lax.ppermute(block, axis, route)]
    gather x4 -> x0, local copies, waits for them, and re-layouts: 6.19 us -> none  [the longest x2 4.2 us: apply_operator(): interior = contract(weights[:5], pieces[:, columns[:, :5], :])]
    unnamed x11 -> x10, local copies, waits for them, and re-layouts: 0.41 us -> 4.2 us
  transfers between devices with their start and end apart: 8 -> 0, of which waited for: 0 -> 0; matrix products, arithmetic and copies ran while one was open for 22% -> 0% of each run, Pallas kernels for 0% -> 0%
where the time goes in v1:
time: 24.9 us; the launch traced here: 24.4 us
  Pallas kernels  20.2 us (81%)
  local copies, waits for them, and re-layouts  4.2 us (17%)
    pallas_call x1, Pallas kernels, body(): pl.pallas_call(functools.partial(kernel, n_dom, n_mode), out_shape=jax.Sh...  20.2 us
    unnamed x10, local copies, waits for them, and re-layouts  4.2 us

profile of v1, /device:TPU:0, one launch (start us, length us, event | category | flops | bytes accessed | tf_op | source)
XLA Modules:
  0.0 24.4 jit_solution(16304914866359846346)
XLA Ops:
  0.0 0.8 %copy.7.cols_ref = s32[64,9]{1,0:T(8,128)S(1)} copy(s32[64,9]{0,1:T(8,128)} %param.11) | data formatting | bytes 4608 | tf_op args[5]
  0.8 0.0 copy-start
  0.8 0.7 %copy-done = f32[4096]{0:T(1024)S(1)} copy-done((f32[4096]{0:T(1024)S(1)}, f32[4096]{0:T(1024)}, u32[]{:S(2)}) %copy-start) | copy-done | bytes 16408
  1.5 0.0 copy-start.1
  1.5 0.7 %copy-done.1 = f32[4096]{0:T(1024)S(1)} copy-done((f32[4096]{0:T(1024)S(1)}, f32[4096]{0:T(1024)}, u32[]{:S(2)}) %copy-start.1) | copy-done | bytes 16408
  2.2 0.0 copy-start.2
  2.2 0.7 %copy-done.2 = f32[16,16]{1,0:T(8,128)S(1)} copy-done((f32[16,16]{1,0:T(8,128)S(1)}, f32[16,16]{1,0:T(8,128)}, u32[]{:S(2)}) %copy-start.2) | copy-done | bytes 1048
  2.9 0.0 copy-start.3
  2.9 0.7 %copy-done.3 = f32[4]{0:T(128)S(1)} copy-done((f32[4]{0:T(128)S(1)}, f32[4]{0:T(128)}, u32[]{:S(2)}) %copy-start.3) | copy-done | bytes 40
  3.6 20.2 %shard_map.64 = f32[32,4,128]{2,1,0:T(4,128)S(1)} custom-call(f32[32,128]{1,0:T(8,128)S(1)} %bitcast.7, f32[32,128]{1,0:T(8,128)S(1)} %bitcast.8, f32[1,4]{1,0:T(1,128)S(1)} %bitcast.9, f32[16,16]{1,0:T(8,128)S(1)} %copy-done.2, f32[9,64,4096]{2,1,0:T(8,128)} %blocks_ref.1, s32[64,9]{1,0:T(8,128)S(1)} %copy.7.cols_ref), custom_call_target="tpu_custom_call" | custom-call | tf_op jit(solution)/shard_map/pallas_call | solution.py:299
  23.8 0.6 %copy.9 = f32[4,4096]{1,0:T(4,128)} copy(f32[4,4096]{1,0:T(4,128)S(1)} %bitcast.6) | data formatting | bytes 131072
Async XLA Ops:
  0.8 0.7 %copy-start = (f32[4096]{0:T(1024)S(1)}, f32[4096]{0:T(1024)}, u32[]{:S(2)}) copy-start(f32[4096]{0:T(1024)} %param.6) | copy-start | bytes 49156
  1.5 0.7 %copy-start.1 = (f32[4096]{0:T(1024)S(1)}, f32[4096]{0:T(1024)}, u32[]{:S(2)}) copy-start(f32[4096]{0:T(1024)} %param.7) | copy-start | bytes 49156
  2.2 0.7 %copy-start.2 = (f32[16,16]{1,0:T(8,128)S(1)}, f32[16,16]{1,0:T(8,128)}, u32[]{:S(2)}) copy-start(f32[16,16]{1,0:T(8,128)} %basis_ref.1) | copy-start | bytes 3076
  2.9 0.7 %copy-start.3 = (f32[4]{0:T(128)S(1)}, f32[4]{0:T(128)}, u32[]{:S(2)}) copy-start(f32[4]{0:T(128)} %param.8) | copy-start | bytes 52

commit v2 on v1

--- a/solution.py
+++ b/solution.py
@@ -44,16 +44,17 @@
 
 def kernel(
     n_dom, n_mode,
-    source_ref, mass_ref, lam_ref, basis_ref, blocks_ref, cols_ref, out_ref,
+    source_hbm, mass_hbm, lam_hbm, basis_hbm, blocks_ref, cols_hbm, out_ref,
+    source_ref, mass_ref, lam_ref, basis_ref, cols_ref,
     own_f32, far_f32, own_hi, own_lo, far_hi, far_lo, v_ref, acc_own, acc_far,
     lam_buf, far1_out, far1_in, far2_out, far2_in, sum1_out, sum1_in, sum2_out, sum2_in,
-    load_sem, lam_send, lam_recv, far1_send, far1_recv, far2_send, far2_recv,
+    small_sem, load_sem, lam_send, lam_recv, far1_send, far1_recv, far2_send, far2_recv,
     sum1_send, sum1_recv, sum2_send, sum2_recv,
 ):
     me = lax.axis_index("dom")
     my_mode = lax.axis_index("mode")
     width = own_f32.shape[1]
-    clusters = cols_ref.shape[0]
+    clusters = cols_ref.shape[1]
     shared = clusters // 2
     md = lam_ref.shape[1]
     levels = out_ref.shape[1]
@@ -62,6 +63,14 @@
     own_chunks = clusters * width // span
     per_chunk = span // width
 
+    small = [
+        pltpu.make_async_copy(src, dst, small_sem.at[n])
+        for n, (src, dst) in enumerate((
+            (source_hbm, source_ref), (mass_hbm, mass_ref), (lam_hbm, lam_ref),
+            (basis_hbm, basis_ref), (cols_hbm, cols_ref)))
+    ]
+    for copy in small:
+        copy.start()
     loads = []
     for n in range(far_chunks):
         lanes = pl.ds(n * span, span)
@@ -80,6 +89,8 @@
     for d in range(1, n_mode):
         pl.semaphore_signal(barrier, inc=1, device_id=(me, lax.rem(my_mode + d, n_mode)), device_id_type=MESH)
 
+    for copy in small:
+        copy.wait()
     f_nat = mass_ref[...] * source_ref[...]
     m_nat = mass_ref[...]
     w_nat = m_nat * f_nat
@@ -165,19 +176,19 @@
                 acc[:, 0:n] = part
         return acc[:, 0:n // 2] + acc[:, n // 2:n]
 
-    cluster_lane = lax.broadcasted_iota(jnp.int32, (clusters, clusters), 1)
+    cluster_row = lax.broadcasted_iota(jnp.int32, (clusters, clusters), 0)
 
     def collect(terms, vectors):
         total = terms[:width]
         high, low = halves(terms[width:])
         moved = None
         for s in range(1, OWN):
-            hot = (cols_ref[:, s:s + 1] == cluster_lane).astype(F32).astype(BF16)
+            hot = (cols_ref[s:s + 1, :] == cluster_row).astype(F32).astype(BF16)
             if vectors == 2:
                 zero = jnp.zeros_like(hot)
                 hot = jnp.concatenate([jnp.concatenate([hot, zero], 1), jnp.concatenate([zero, hot], 1)], 0)
             rows = slice((s - 1) * width, s * width)
-            part = dot(high[rows], hot) + dot(low[rows], hot)
+            part = dot(high[rows], hot, ((1,), (1,))) + dot(low[rows], hot, ((1,), (1,)))
             moved = part if moved is None else moved + part
         return total + moved
 
@@ -294,14 +305,20 @@
         levels = LEVELS // n_mode
         lines = vertices // 128
         vmem = pl.BlockSpec(memory_space=pltpu.VMEM)
+        hbm = pl.BlockSpec(memory_space=pltpu.HBM)
         dma = pltpu.SemaphoreType.DMA
         chunks = vertices // 1024 + shared * width // 1024
         result = pl.pallas_call(
             functools.partial(kernel, n_dom, n_mode),
             out_shape=jax.ShapeDtypeStruct((lines, levels, 128), F32),
-            in_specs=[vmem, vmem, vmem, vmem, pl.BlockSpec(memory_space=pl.ANY), vmem],
+            in_specs=[hbm] * 6,
             out_specs=vmem,
             scratch_shapes=[
+                pltpu.VMEM((lines, 128), F32),
+                pltpu.VMEM((lines, 128), F32),
+                pltpu.VMEM((1, md), F32),
+                pltpu.VMEM(trace_basis.shape, F32),
+                pltpu.VMEM((slots, clusters), jnp.int32),
                 pltpu.VMEM((OWN, width, vertices), F32),
                 pltpu.VMEM((slots - OWN, width, shared * width), F32),
                 pltpu.VMEM((OWN * width, vertices), BF16),
@@ -320,16 +337,17 @@
                 pltpu.VMEM((n_dom - 1, 8, 128), F32),
                 pltpu.VMEM((2 * md * n_mode, 128), F32),
                 pltpu.VMEM((n_dom - 1, 2 * md * n_mode, 128), F32),
+                dma((5,)),
                 dma((chunks,)),
                 dma((n_mode,)), dma((n_mode,)),
                 dma((4,)), dma((4,)), dma((4,)), dma((4,)),
                 dma((n_dom - 1,)), dma((n_dom - 1,)), dma((n_dom - 1,)), dma((n_dom - 1,)),
             ],
             compiler_params=pltpu.CompilerParams(
-                collective_id=0, has_side_effects=True, vmem_limit_bytes=48 * 1024 * 1024),
+                collective_id=0, has_side_effects=True, vmem_limit_bytes=64 * 1024 * 1024),
         )(
             source.reshape(lines, 128), mass.reshape(lines, 128), lambdas.reshape(1, md),
-            trace_basis, blocks, columns,
+            trace_basis, blocks, columns.T,
         )
         return jnp.transpose(result, (1, 0, 2)).reshape(levels, vertices)
 

time: 24.9 us -> 22.6 us (0.908); the launches traced: 24.4 us -> 22.4 us
  local copies, waits for them, and re-layouts: 4.2 us -> 1.47 us
  Pallas kernels: 20.2 us -> 20.9 us
    unnamed x10 -> x1, local copies, waits for them, and re-layouts: 4.2 us -> 1.47 us
    pallas_call x1, Pallas kernels: 20.2 us -> 20.9 us  [body(): pl.pallas_call(functools.partial(kernel, n_dom, n_mode), out_shape=jax.Sh...]
where the time goes in v2:
time: 22.6 us; the launch traced here: 22.4 us
  Pallas kernels  20.9 us (92%)
  local copies, waits for them, and re-layouts  1.47 us (7%)
    pallas_call x1, Pallas kernels, body(): pl.pallas_call(functools.partial(kernel, n_dom, n_mode), out_shape=jax.Sh...  20.9 us
    unnamed x1, local copies, waits for them, and re-layouts  1.47 us

profile of v2, /device:TPU:0, one launch (start us, length us, event | category | flops | bytes accessed | tf_op | source)
XLA Modules:
  0.0 22.4 jit_solution(1277198640582580415)
XLA Ops:
  0.0 20.9 %shard_map.64 = f32[32,4,128]{2,1,0:T(4,128)} custom-call(f32[32,128]{1,0:T(8,128)} %bitcast.8, f32[32,128]{1,0:T(8,128)} %bitcast.9, f32[1,4]{1,0:T(1,128)} %bitcast.11, f32[16,16]{1,0:T(8,128)} %basis_hbm.1, f32[9,64,4096]{2,1,0:T(8,128)} %blocks_ref.1, s32[9,64]{1,0:T(8,128)} %bitcast.10), custom_call_target="tpu_custom_call" | custom-call | tf_op jit(solution)/shard_map/pallas_call | solution.py:311
  20.9 1.5 %copy.8 = f32[4,4096]{1,0:T(4,128)} copy(f32[4,4096]{1,0:T(4,128)} %bitcast.7) | data formatting | bytes 131072

commit v3 on v2

--- a/solution.py
+++ b/solution.py
@@ -33,6 +33,12 @@
 def unfold(value):
     half = value.shape[1] // 2
     return jnp.concatenate([value[:, :half], value[:, half:]], axis=0)
+
+
+def row_of(column):
+    n = column.shape[0]
+    eye = lax.broadcasted_iota(jnp.int32, (n, n), 0) == lax.broadcasted_iota(jnp.int32, (n, n), 1)
+    return jnp.sum(jnp.where(eye, jnp.broadcast_to(column[:, 0:1], (n, n)), 0.0), axis=0, keepdims=True)
 
 
 def column_of(row):
@@ -59,6 +65,7 @@
     md = lam_ref.shape[1]
     levels = out_ref.shape[1]
     span = 1024
+    modes = md * n_mode
     far_chunks = shared * width // span
     own_chunks = clusters * width // span
     per_chunk = span // width
@@ -84,10 +91,10 @@
         load.start()
 
     barrier = pltpu.get_barrier_semaphore()
+    for d in range(1, n_mode):
+        pl.semaphore_signal(barrier, inc=1, device_id=(me, lax.rem(my_mode + d, n_mode)), device_id_type=MESH)
     for d in range(1, n_dom):
         pl.semaphore_signal(barrier, inc=1, device_id=(lax.rem(me + d, n_dom), my_mode), device_id_type=MESH)
-    for d in range(1, n_mode):
-        pl.semaphore_signal(barrier, inc=1, device_id=(me, lax.rem(my_mode + d, n_mode)), device_id_type=MESH)
 
     for copy in small:
         copy.wait()
@@ -114,7 +121,7 @@
     f_t = across(f_nat)
     w_t = m_t * f_t
 
-    def spread(vectors):
+    def spread(vectors, first, last):
         high = [v.astype(BF16).astype(F32) for v in vectors]
         packed = jnp.concatenate(high + [v - h for v, h in zip(vectors, high)], axis=1)
         lane = lax.rem(lax.broadcasted_iota(jnp.int32, packed.shape, 1), clusters)
@@ -123,25 +130,13 @@
         def place(g, carry):
             v_ref[pl.ds(pl.multiple_of(g * width, width), width), 0:n] = jnp.where(lane == g, packed, 0.0).astype(BF16)
             return carry
-        lax.fori_loop(0, clusters, place, 0, unroll=8)
-
-    spread([f_t, w_t])
+        lax.fori_loop(first, last, place, 0, unroll=8)
+
+    spread([f_t, w_t], 0, clusters)
 
     lam_row = lam_ref[...]
     lam_tile = jnp.concatenate([column_of(lam_row), jnp.zeros((8 - md, 128), F32)], axis=0)
     lam_buf[0] = lam_tile
-    wait_for = n_dom - 1 + n_mode - 1
-    pl.semaphore_wait(barrier, wait_for)
-
-    sends = []
-    lam_copies = []
-    for d in range(1, n_mode):
-        copy = pltpu.make_async_remote_copy(
-            src_ref=lam_buf.at[0], dst_ref=lam_buf.at[d], send_sem=lam_send.at[d], recv_sem=lam_recv.at[d],
-            device_id=(me, lax.rem(my_mode + d, n_mode)), device_id_type=MESH)
-        copy.start()
-        lam_copies.append(copy)
-
     def far_copies(out_buf, in_buf, send, recv):
         copies = []
         for h, offset in enumerate(OFFSETS):
@@ -202,7 +197,17 @@
         rows = terms[h * width:(h + 1) * width]
         both = jnp.concatenate([rows[:, :shared], rows[:, clusters:clusters + shared]], axis=1)
         far1_out[h] = fold(both)
-        far1[h].start()
+    wait_for = n_dom - 1 + n_mode - 1
+    pl.semaphore_wait(barrier, wait_for)
+    for copy in far1:
+        copy.start()
+    lam_copies = []
+    for d in range(1, n_mode):
+        copy = pltpu.make_async_remote_copy(
+            src_ref=lam_buf.at[0], dst_ref=lam_buf.at[d], send_sem=lam_send.at[d], recv_sem=lam_recv.at[d],
+            device_id=(me, lax.rem(my_mode + d, n_mode)), device_id_type=MESH)
+        copy.start()
+        lam_copies.append(copy)
     terms = product(OWN, own_chunks, far_chunks, own_f32, own_hi, own_lo, acc_own, n1, True)
     image = collect(terms, 2)
     for h in range(4):
@@ -211,24 +216,26 @@
     u_t = image[:, :clusters] + widen(arrived[:, :shared])
     q_t = image[:, clusters:] + widen(arrived[:, shared:])
 
-    f_v, w_v, m_v, u_v, q_v = fold(f_t), fold(w_t), fold(m_t), fold(u_t), fold(q_t)
-
-    def over(value):
-        return jnp.sum(value, axis=0, keepdims=True)
-
-    sum1_out[...] = jnp.concatenate(
-        [over(f_v * f_v), over(f_v * u_v), over(f_v * w_v), jnp.zeros((5, 128), F32)], axis=0)
-    sum1 = sum_copies(sum1_out, sum1_in, sum1_send, sum1_recv)
-    for copy in sum1:
-        copy.start()
-
     n2 = 2 * clusters
-    spread([u_t])
+    spread([u_t], 0, shared)
     terms = product(4, far_chunks, 0, far_f32, far_hi, far_lo, acc_far, n2, False)
     far2 = far_copies(far2_out, far2_in, far2_send, far2_recv)
     for h in range(4):
         far2_out[h] = fold(fold(terms[h * width:(h + 1) * width, :shared]))
         far2[h].start()
+
+    f_v, w_v, m_v, u_v, q_v = fold(f_t), fold(w_t), fold(m_t), fold(u_t), fold(q_t)
+
+    def over(value):
+        return jnp.sum(value, axis=0, keepdims=True)
+
+    sum1_out[...] = jnp.concatenate(
+        [over(f_v * f_v), over(f_v * u_v), over(f_v * w_v), jnp.zeros((5, 128), F32)], axis=0)
+    sum1 = sum_copies(sum1_out, sum1_in, sum1_send, sum1_recv)
+    for copy in sum1:
+        copy.start()
+
+    spread([u_t], shared, clusters)
     terms = product(OWN, own_chunks, far_chunks, own_f32, own_hi, own_lo, acc_own, n2, False)
     image = collect(terms, 1)
 
@@ -265,30 +272,38 @@
         image_r = u_v - a * p_v - al * q_v + lam[k:k + 1] * (m_v * r)
         squares.append(over(r * r))
         curves.append(over(r * image_r))
-    sum2_out[...] = jnp.concatenate(squares + curves, axis=0)
+    sum2_out[...] = jnp.zeros((8, 128), F32)
+    for row, parts in enumerate((squares, curves)):
+        column = jnp.sum(jnp.concatenate(parts, axis=0), axis=1, keepdims=True)
+        sum2_out[row:row + 1, 0:modes] = row_of(column)
     sum2 = sum_copies(sum2_out, sum2_in, sum2_send, sum2_recv)
     for copy in sum2:
         copy.start()
 
     u_nat = back(u_t)
-    rows = [column_of(basis_ref[pl.ds(my_mode * levels + level, 1), :]) for level in range(levels)]
+    basis_own = jnp.concatenate(
+        [basis_ref[pl.ds(my_mode * levels + level, 1), :] for level in range(levels)], axis=0)
+    t_row = basis_ref[0:1, :]
+    t2_row = t_row * t_row
+    alpha_row, rr0_row, lam_row = row_of(alpha), row_of(rr0), row_of(lam)
 
     for copy in sum2:
         copy.wait_recv()
     sums = sum2_out[...]
     for d in range(n_dom - 1):
         sums = sums + sum2_in[d]
-    modes = md * n_mode
-    sums = jnp.broadcast_to(jnp.sum(sums, axis=1, keepdims=True), (2 * modes, 128))
-    rr1 = t2 * sums[:modes]
-    beta = rr1 / rr0
-    alpha1 = rr1 / (t2 * sums[modes:] - beta * (rr1 / alpha))
-    coef_f = t * (alpha + alpha1 * (1.0 + beta))
-    coef_u = -t * (alpha1 * alpha)
-    coef_w = coef_u * lam
+    rr1 = t2_row * sums[0:1, 0:modes]
+    beta = rr1 / rr0_row
+    alpha1 = rr1 / (t2_row * sums[1:2, 0:modes] - beta * (rr1 / alpha_row))
+    coef_f = t_row * (alpha_row + alpha1 * (1.0 + beta))
+    coef_u = -t_row * (alpha1 * alpha_row)
+    coef_w = coef_u * lam_row
+    c_f, c_u, c_w = (
+        jnp.broadcast_to(jnp.sum(basis_own * c, axis=1, keepdims=True), (levels, 128))
+        for c in (coef_f, coef_u, coef_w))
     for level in range(levels):
-        c_f, c_u, c_w = (over(rows[level] * c) for c in (coef_f, coef_u, coef_w))
-        out_ref[:, level, :] = c_f * f_nat + c_u * u_nat + c_w * w_nat
+        one = slice(level, level + 1)
+        out_ref[:, level, :] = c_f[one] * f_nat + c_u[one] * u_nat + c_w[one] * w_nat
 
     for copy in lam_copies + far1 + far2 + sum1 + sum2:
         copy.wait_send()
@@ -335,8 +350,8 @@
                 pltpu.VMEM((4, width // 4, 4 * shared), F32),
                 pltpu.VMEM((8, 128), F32),
                 pltpu.VMEM((n_dom - 1, 8, 128), F32),
-                pltpu.VMEM((2 * md * n_mode, 128), F32),
-                pltpu.VMEM((n_dom - 1, 2 * md * n_mode, 128), F32),
+                pltpu.VMEM((8, 128), F32),
+                pltpu.VMEM((n_dom - 1, 8, 128), F32),
                 dma((5,)),
                 dma((chunks,)),
                 dma((n_mode,)), dma((n_mode,)),
@@ -344,7 +359,7 @@
                 dma((n_dom - 1,)), dma((n_dom - 1,)), dma((n_dom - 1,)), dma((n_dom - 1,)),
             ],
             compiler_params=pltpu.CompilerParams(
-                collective_id=0, has_side_effects=True, vmem_limit_bytes=64 * 1024 * 1024),
+                collective_id=0, has_side_effects=True, vmem_limit_bytes=64 * 1024 * 1024 - 131072),
         )(
             source.reshape(lines, 128), mass.reshape(lines, 128), lambdas.reshape(1, md),
             trace_basis, blocks, columns.T,

time: 22.6 us -> 22.5 us (level)
  no operation moved by 1% of the time
where the time goes in v3:
time: 22.5 us; the launch traced here: 22.3 us
  Pallas kernels  20.8 us (92%)
  local copies, waits for them, and re-layouts  1.47 us (7%)
    pallas_call x1, Pallas kernels, body(): pl.pallas_call(functools.partial(kernel, n_dom, n_mode), out_shape=jax.Sh...  20.8 us
    unnamed x1, local copies, waits for them, and re-layouts  1.47 us

profile of v3, /device:TPU:0, one launch (start us, length us, event | category | flops | bytes accessed | tf_op | source)
XLA Modules:
  0.0 22.3 jit_solution(16580129009471141639)
XLA Ops:
  0.0 20.8 %shard_map.64 = f32[32,4,128]{2,1,0:T(4,128)} custom-call(f32[32,128]{1,0:T(8,128)} %bitcast.8, f32[32,128]{1,0:T(8,128)} %bitcast.9, f32[1,4]{1,0:T(1,128)} %bitcast.11, f32[16,16]{1,0:T(8,128)} %basis_hbm.1, f32[9,64,4096]{2,1,0:T(8,128)} %blocks_ref.1, s32[9,64]{1,0:T(8,128)} %bitcast.10), custom_call_target="tpu_custom_call" | custom-call | tf_op jit(solution)/shard_map/pallas_call | solution.py:326
  20.9 1.5 %copy.8 = f32[4,4096]{1,0:T(4,128)} copy(f32[4,4096]{1,0:T(4,128)} %bitcast.7) | data formatting | bytes 131072

commit v4 on v3

--- a/solution.py
+++ b/solution.py
@@ -325,7 +325,7 @@
         chunks = vertices // 1024 + shared * width // 1024
         result = pl.pallas_call(
             functools.partial(kernel, n_dom, n_mode),
-            out_shape=jax.ShapeDtypeStruct((lines, levels, 128), F32),
+            out_shape=pltpu.VMEM((lines, levels, 128), F32),
             in_specs=[hbm] * 6,
             out_specs=vmem,
             scratch_shapes=[
@@ -359,7 +359,7 @@
                 dma((n_dom - 1,)), dma((n_dom - 1,)), dma((n_dom - 1,)), dma((n_dom - 1,)),
             ],
             compiler_params=pltpu.CompilerParams(
-                collective_id=0, has_side_effects=True, vmem_limit_bytes=64 * 1024 * 1024 - 131072),
+                collective_id=0, has_side_effects=True, vmem_limit_bytes=64 * 1024 * 1024 - 262144),
         )(
             source.reshape(lines, 128), mass.reshape(lines, 128), lambdas.reshape(1, md),
             trace_basis, blocks, columns.T,

time: 22.5 us -> 21 us (0.933)
  local copies, waits for them, and re-layouts: 1.47 us -> 0.63 us
  Pallas kernels: 20.8 us -> 20.2 us
    unnamed x1, local copies, waits for them, and re-layouts: 1.47 us -> 0.63 us
    pallas_call x1, Pallas kernels: 20.8 us -> 20.2 us  [body(): pl.pallas_call(functools.partial(kernel, n_dom, n_mode), out_shape=pltpu....]
where the time goes in v4:
time: 21 us; the launch traced here: 20.9 us
  Pallas kernels  20.2 us (96%)
  local copies, waits for them, and re-layouts  0.63 us (3%)
    pallas_call x1, Pallas kernels, body(): pl.pallas_call(functools.partial(kernel, n_dom, n_mode), out_shape=pltpu....  20.2 us
    unnamed x1, local copies, waits for them, and re-layouts  0.63 us

profile of v4, /device:TPU:0, one launch (start us, length us, event | category | flops | bytes accessed | tf_op | source)
XLA Modules:
  0.0 20.9 jit_solution(9365498414873382611)
XLA Ops:
  0.0 20.2 %shard_map.64 = f32[32,4,128]{2,1,0:T(4,128)S(1)} custom-call(f32[32,128]{1,0:T(8,128)} %bitcast.8, f32[32,128]{1,0:T(8,128)} %bitcast.9, f32[1,4]{1,0:T(1,128)} %bitcast.11, f32[16,16]{1,0:T(8,128)} %basis_hbm.1, f32[9,64,4096]{2,1,0:T(8,128)} %blocks_ref.1, s32[9,64]{1,0:T(8,128)} %bitcast.10), custom_call_target="tpu_custom_call" | custom-call | tf_op jit(solution)/shard_map/pallas_call | solution.py:326
  20.2 0.6 %copy.8 = f32[4,4096]{1,0:T(4,128)} copy(f32[4,4096]{1,0:T(4,128)S(1)} %bitcast.7) | data formatting | bytes 131072

commit v5 on v4

--- a/solution.py
+++ b/solution.py
@@ -260,18 +260,20 @@
     alpha = rr0 / (t2 * (sums[1:2] + lam * sums[2:3]))
     alpha_lam = alpha * lam
 
+    residuals, squares, curves = [], [], []
+    for k in range(modes):
+        a, al = alpha[k:k + 1], alpha_lam[k:k + 1]
+        r = f_v - a * u_v - al * w_v
+        residuals.append((r, u_v - al * q_v + lam[k:k + 1] * (m_v * r)))
+        squares.append(over(r * r))
+
     for h in range(4):
         far2[h].wait_recv()
     arrived = unfold(unfold(far2_in[0] + far2_in[1] + far2_in[2] + far2_in[3]))
     p_v = fold(image + widen(arrived))
 
-    squares, curves = [], []
-    for k in range(md * n_mode):
-        a, al = alpha[k:k + 1], alpha_lam[k:k + 1]
-        r = f_v - a * u_v - al * w_v
-        image_r = u_v - a * p_v - al * q_v + lam[k:k + 1] * (m_v * r)
-        squares.append(over(r * r))
-        curves.append(over(r * image_r))
+    for k, (r, partial) in enumerate(residuals):
+        curves.append(over(r * (partial - alpha[k:k + 1] * p_v)))
     sum2_out[...] = jnp.zeros((8, 128), F32)
     for row, parts in enumerate((squares, curves)):
         column = jnp.sum(jnp.concatenate(parts, axis=0), axis=1, keepdims=True)

time: 21 us -> 21.1 us (level)
  no operation moved by 1% of the time
where the time goes in v5:
time: 21.1 us; the launch traced here: 20.9 us
  Pallas kernels  20.3 us (96%)
  local copies, waits for them, and re-layouts  0.63 us (3%)
    pallas_call x1, Pallas kernels, body(): pl.pallas_call(functools.partial(kernel, n_dom, n_mode), out_shape=pltpu....  20.3 us
    unnamed x1, local copies, waits for them, and re-layouts  0.63 us

profile of v5, /device:TPU:0, one launch (start us, length us, event | category | flops | bytes accessed | tf_op | source)
XLA Modules:
  0.0 20.9 jit_solution(6142422218479524986)
XLA Ops:
  0.0 20.3 %shard_map.64 = f32[32,4,128]{2,1,0:T(4,128)S(1)} custom-call(f32[32,128]{1,0:T(8,128)} %bitcast.8, f32[32,128]{1,0:T(8,128)} %bitcast.9, f32[1,4]{1,0:T(1,128)} %bitcast.11, f32[16,16]{1,0:T(8,128)} %basis_hbm.1, f32[9,64,4096]{2,1,0:T(8,128)} %blocks_ref.1, s32[9,64]{1,0:T(8,128)} %bitcast.10), custom_call_target="tpu_custom_call" | custom-call | tf_op jit(solution)/shard_map/pallas_call | solution.py:328
  20.3 0.6 %copy.8 = f32[4,4096]{1,0:T(4,128)} copy(f32[4,4096]{1,0:T(4,128)S(1)} %bitcast.7) | data formatting | bytes 131072
